TPU v7x, 512 devices: a whole 4x4x16 slice. The times are simulated.
512 devices in a mesh: ens: 8 (over y_lo, x), slab: 64 (over y_hi, z, core).
Axes of the slice: x: 4, y: 4 (y_hi: 2, y_lo: 2; y = y_hi * 2 + y_lo), z: 16, core: 2. Of those that a mesh axis runs over, the one named last changes fastest.
Arguments:
- state: float32 [64, 64, 1024], P('slab'), may hold values from -6 to 6
- face_coefs: bfloat16 [2, 64, 64, 1024], P(None, 'slab'), may hold values from 0.019897461 to 0.19921875
- codes: int32 [8], P('ens'), may hold values from 0 to 999999
- acoustic_inv: float32 [64, 64, 64], P('slab')
- bounds: int32 [5], replicated, may hold values from 0 to 64, as said below
- land_mask: int32 [64, 1024], P('slab'), may hold values 0 or 1
- target: bfloat16 [64, 64, 1024], P(None, 'slab'), may hold values from -6 to 6
- w_in: bfloat16 [64, 1024], replicated, may hold values from -0.75 to 0.75
- bias_in: float32 [1024], replicated, may hold values from -3 to 3
- land_weight: float32 [1024], replicated, may hold values from -4 to 4
- w_out: bfloat16 [1024, 64], replicated, may hold values from -0.1875 to 0.1875
- bias_out: float32 [64], replicated, may hold values from -3 to 3
Outputs:
- upd_in: float32 [64, 1024], replicated
- upd_out: float32 [1024, 64], replicated
- grad_state: float32 [64, 64, 1024], P('slab')
Inputs may be any that keep to these rules, and one draw needn't show every extreme that they name: bounds[0] = 0 and bounds[4] = 64; the entries rise strictly.
All inputs are finite; a program needn't handle non-finite values. No bound on the sum of `land_mask` on one device may be relied on, other than what follows from the above.
Results may differ from a plain program's by a relative error of at most 0.0004.
The roundings to bfloat16 on the way count: a program that leaves them out, or rounds other values in their place, can miss the bound.
Values sent between devices are 32-bit elements; how exact they have to be, the bound alone decides.
A program may use at most 64 MiB of HBM per device.

v0:
```python
import jax
import jax.numpy as jnp
from jax import lax
from jax.sharding import PartitionSpec as P


def noise(code, cell):
    mult = code % 251 + 2
    first = (mult * (cell % 65521) + 12345) % 65521
    second = (first * 31337 + mult) % 65521
    return second.astype(jnp.float32) / 65521.0 - 0.5


def diffuse(field, east, north):
    flux_x = east * (jnp.roll(field, -1, axis=2) - field)
    step_y = jnp.concatenate([field[:, 1:] - field[:, :-1], jnp.zeros_like(field[:, :1])], axis=1)
    flux_y = north * step_y
    lower = jnp.concatenate([jnp.zeros_like(flux_y[:, :1]), flux_y[:, :-1]], axis=1)
    return field + flux_x - jnp.roll(flux_x, 1, axis=2) + flux_y - lower


def column_step(
    x_row, land_row, target_row, solve_row, w_in, bias_in, land_weight, w_out, bias_out, scale
):
    pre = lax.dot_general(w_in, x_row, (((0,), (0,)), ((), ())), preferred_element_type=jnp.float32)
    pre = pre + bias_in[:, None] + land_weight[:, None] * land_row[None, :]
    sig = jax.nn.sigmoid(pre)
    hidden = (pre * sig).astype(jnp.bfloat16)
    out = lax.dot_general(
        w_out, hidden, (((0,), (0,)), ((), ())), preferred_element_type=jnp.float32
    )
    out = out + bias_out[:, None]
    d_out = ((out - target_row.astype(jnp.float32)) * scale).astype(jnp.bfloat16)
    g_out = lax.dot_general(
        hidden, d_out, (((1,), (1,)), ((), ())), preferred_element_type=jnp.float32
    )
    d_hidden = jnp.dot(w_out, d_out, preferred_element_type=jnp.float32)
    d_pre = (d_hidden * sig * (1.0 + pre * (1.0 - sig))).astype(jnp.bfloat16)
    g_in = lax.dot_general(
        x_row, d_pre, (((1,), (1,)), ((), ())), preferred_element_type=jnp.float32
    )
    d_x = jnp.dot(w_in, d_pre, preferred_element_type=jnp.float32)
    d_h = lax.dot_general(solve_row, d_x, (((0,), (0,)), ((), ())), precision=lax.Precision.HIGHEST)
    return (g_in, g_out, d_h)


def normalized(grad):
    return grad / jnp.sqrt(jnp.mean(grad * grad) + 1e-06)


def on_device(
    state,
    face_coefs,
    codes,
    acoustic_inv,
    bounds,
    land_mask,
    target,
    w_in,
    bias_in,
    land_weight,
    w_out,
    bias_out,
):
    lev_local, lat_count, lon_count = state.shape
    level_count = w_in.shape[0]
    hidden_count = w_in.shape[1]
    lat_local = land_mask.shape[0]
    block_count = bounds.shape[0] - 1
    east = face_coefs[0].astype(jnp.float32)
    north = face_coefs[1].astype(jnp.float32)
    first_level = lax.axis_index("slab") * lev_local
    level_ids = first_level + jnp.arange(lev_local, dtype=jnp.int32)
    lat_ids = jnp.arange(lat_count, dtype=jnp.int32)
    lon_ids = jnp.arange(lon_count, dtype=jnp.int32)
    cell = (level_ids[:, None, None] * lat_count + lat_ids[None, :, None]) * lon_count + lon_ids[
        None, None, :
    ]
    fresh = diffuse(state + noise(codes[0], cell), east, north)
    columns = lax.all_to_all(fresh, "slab", split_axis=1, concat_axis=0, tiled=True)
    level = jnp.arange(level_count, dtype=jnp.int32)
    block = jnp.sum((level[:, None] >= bounds[None, 1:block_count]).astype(jnp.int32), axis=1)
    couple = (block[:, None] == block[None, :]).astype(jnp.float32)
    solve_mat = acoustic_inv * couple[None]
    land = land_mask.astype(jnp.float32)
    scale = 1.0 / lax.axis_size("ens")

    def per_row(row, carry):
        acc_in, acc_out, back = carry
        source = lax.dynamic_index_in_dim(columns, row, 1, keepdims=False)
        solve_row = lax.dynamic_index_in_dim(solve_mat, row, 0, keepdims=False)
        x_row = jnp.dot(solve_row, source, precision=lax.Precision.HIGHEST).astype(jnp.bfloat16)
        land_row = lax.dynamic_index_in_dim(land, row, 0, keepdims=False)
        target_row = lax.dynamic_index_in_dim(target, row, 1, keepdims=False)
        part_in, part_out, d_h = column_step(
            x_row,
            land_row,
            target_row,
            solve_row,
            w_in,
            bias_in,
            land_weight,
            w_out,
            bias_out,
            scale,
        )
        back = d_h[:, None, :]
        return (acc_in + part_in, acc_out + part_out, back)

    start = (
        jnp.zeros((level_count, hidden_count), jnp.float32),
        jnp.zeros((hidden_count, level_count), jnp.float32),
        jnp.zeros((level_count, lat_local, lon_count), jnp.float32),
    )
    g_in, g_out, back = lax.fori_loop(0, lat_local, per_row, start)
    g_in, g_out = lax.psum((g_in, g_out), ("ens", "slab"))
    returned = lax.all_to_all(back, "slab", split_axis=0, concat_axis=1, tiled=True)
    summed = lax.psum(returned, "ens")
    grad_state = diffuse(summed, east, north)
    return (normalized(g_in), normalized(g_out), grad_state)


def solution(mesh):
    placed = (
        P("slab", None, None),
        P(None, "slab", None, None),
        P("ens"),
        P("slab", None, None),
        P(),
        P("slab", None),
        P(None, "slab", None),
        P(),
        P(),
        P(),
        P(),
        P(),
    )
    return jax.shard_map(
        on_device,
        mesh=mesh,
        in_specs=placed,
        out_specs=(P(), P(), P("slab", None, None)),
        check_vma=False,
    )
```

profile of v0, /device:TPU:32, one launch (start us, length us, event | category | flops | bytes accessed | tf_op | source)
XLA Modules:
  0.0 652.6 jit_solution(9690819280671128844)
XLA Ops:
  8.0 0.0 copy-start
  8.0 0.0 copy-start.2
  8.8 4.9 fusion.15
  13.7 0.2 slice_subtract_fusion.1
  13.9 0.6 slice.72
  14.5 1.0 fusion.36
  15.5 5.8 fusion.16
  21.3 0.1 slice.74
  21.5 0.0 copy-done.2
  21.5 5.2 fusion.18
  26.7 18.4 %all-to-all-start = ((f32[1,64,1024]{2,0,1:T(1,128)}), f32[1,64,1024]{2,0,1:T(1,128)S(1)}, u32[]{:S(2)}, u32[]{:S(2)}) async-start(f32[1,64,1024]{2,0,1:T(1,128)} %fusion.18), calls=%async_computation | async-start | bytes 524288 | tf_op jit(solution)/shard_map/all_to_all | solution.py:80
  45.1 0.1 slice.55
  45.2 0.1 convert_reduce_fusion
  45.3 22.7 %all-to-all-done = f32[1,64,1024]{2,0,1:T(1,128)S(1)} async-done(((f32[1,64,1024]{2,0,1:T(1,128)}), f32[1,64,1024]{2,0,1:T(1,128)S(1)}, u32[]{:S(2)}, u32[]{:S(2)}) %all-to-all-start) | async-done | bytes 262176 | tf_op jit(solution)/shard_map/all_to_all | solution.py:80
  68.0 0.4 convolution_convert_fusion
  68.4 0.0 copy-start.5
  68.4 0.0 copy-start.6
  68.4 0.0 copy-start.8
  68.5 1.4 multiply_convert_fusion
  69.9 0.8 fusion.5
  70.7 0.5 copy-done.1
  71.2 2.1 fusion.1
  73.4 0.8 fusion.38
  74.1 0.5 convolution_bitcast_fusion
  74.6 1.0 copy.23
  75.6 4.9 all-to-all-start.1
  80.5 0.0 all-reduce.10.cloned.1.call-start
  80.5 2.8 fusion.39
  83.3 1.2 fusion.37
  84.5 0.0 all-reduce.10.cloned.1.call-update
  84.5 0.2 all-reduce.8.cloned.1.call-start
  84.7 459.8 %all-reduce.10.cloned.1.call-done = (f32[64,1024]{1,0:T(8,128)}, f32[1024,64]{0,1:T(8,128)}) async-done(((f32[64,1024]{1,0:T(8,128)}, f32[1024,64]{0,1:T(8,128)}), (f32[64,1024]{1,0:T(8,128)}, f32[1024,64]{0,1:T(8,128)})) %all-reduce.10.cloned.1.call-update) | async-done | bytes 524304 | tf_op jit(solution)/shard_map/psum | solution.py:116
  544.6 1.6 multiply_reduce_fusion.1
  546.9 1.7 broadcast_divide_fusion.1
  548.6 0.0 all-to-all-done.1
  548.6 0.7 copy-done.3
  549.3 0.0 all-reduce.8.cloned.1.call-update
  549.3 1.6 multiply_reduce_fusion
  551.6 1.7 broadcast_divide_fusion
  553.3 83.9 %all-reduce.8.cloned.1.call-done = f32[1,64,1024]{2,0,1:T(1,128)} async-done(((f32[1,64,1024]{2,0,1:T(1,128)}), f32[1,64,1024]{2,0,1:T(1,128)}) %all-reduce.8.cloned.1.call-update) | async-done | bytes 262160 | tf_op jit(solution)/shard_map/psum | solution.py:118
  637.2 1.3 slice_subtract_fusion
  638.6 0.3 pad_multiply_fusion
  638.9 0.8 slice.80
  639.6 1.6 slice.79
  641.2 1.4 fusion.19
  642.6 0.1 slice.81
  642.7 1.7 fusion.21
  644.4 0.8 copy.24
  (21 shorter events, 0.1 us)
Async XLA Ops:
  8.0 60.4 %copy-start = (bf16[64,1024]{1,0:T(8,128)(2,1)S(1)}, bf16[64,1024]{1,0:T(8,128)(2,1)}, u32[]{:S(2)}) copy-start(bf16[64,1024]{1,0:T(8,128)(2,1)} %param.19) | copy-start | bytes 393220
  8.0 13.5 %copy-start.2 = (f32[1,64,1024]{2,1,0:T(8,128)S(1)}, f32[1,64,1024]{2,1,0:T(8,128)}, u32[]{:S(2)}) copy-start(f32[1,64,1024]{2,1,0:T(8,128)} %param.12) | copy-start | bytes 786436
  8.0 37.1 %copy-start.11 = (s32[5]{0:T(128)S(1)}, s32[5]{0:T(128)}, u32[]{:S(2)}) copy-start(s32[5]{0:T(128)} %param.16) | copy-start | bytes 64
  8.0 37.1 %copy-start.7 = (s32[1,1024]{1,0:T(1,128)S(1)}, s32[1,1024]{1,0:T(1,128)}, u32[]{:S(2)}) copy-start(s32[1,1024]{1,0:T(1,128)} %param.17) | copy-start | bytes 12292
  8.0 59.9 %copy-start.4 = (f32[1,64,64]{2,1,0:T(8,128)S(1)}, f32[1,64,64]{2,1,0:T(8,128)}, u32[]{:S(2)}) copy-start(f32[1,64,64]{2,1,0:T(8,128)} %param.15) | copy-start | bytes 49156
  8.1 60.3 %copy-start.9 = (f32[1024]{0:T(1024)S(1)}, f32[1024]{0:T(1024)}, u32[]{:S(2)}) copy-start(f32[1024]{0:T(1024)} %param.21) | copy-start | bytes 12292
  8.1 60.3 %copy-start.10 = (f32[1024]{0:T(1024)S(1)}, f32[1024]{0:T(1024)}, u32[]{:S(2)}) copy-start(f32[1024]{0:T(1024)} %param.20) | copy-start | bytes 12292
  26.7 41.3 %all-to-all-start = ((f32[1,64,1024]{2,0,1:T(1,128)}), f32[1,64,1024]{2,0,1:T(1,128)S(1)}, u32[]{:S(2)}, u32[]{:S(2)}) async-start(f32[1,64,1024]{2,0,1:T(1,128)} %fusion.18), calls=%async_computation | async-start | bytes 524288 | tf_op jit(solution)/shard_map/all_to_all | solution.py:80
  68.4 1.5 copy-start.5
  68.4 1.5 copy-start.6
  68.4 1.5 copy-start.8
  69.9 1.3 copy-start.1
  75.6 473.0 %all-to-all-start.1 = ((f32[64,1,1024]{2,1,0:T(1,128)}), f32[64,1,1024]{2,1,0:T(1,128)S(1)}, u32[]{:S(2)}, u32[]{:S(2)}) async-start(f32[64,1,1024]{2,1,0:T(1,128)} %copy.23), calls=%async_computation.1 | async-start | bytes 524288 | tf_op jit(solution)/shard_map/all_to_all | solution.py:117
  80.5 464.1 %all-reduce.10.cloned.1.call-start = ((), (), s32[]{:S(2)}) async-start(), calls=%async_computation.3 | async-start | bytes 1048576 | tf_op jit(solution)/shard_map/psum | solution.py:116
  84.5 552.7 %all-reduce.8.cloned.1.call-start = ((), (), s32[]{:S(2)}) async-start(), calls=%async_computation.2 | async-start | bytes 524288 | tf_op jit(solution)/shard_map/psum | solution.py:118
  548.6 0.7 copy-start.3
Sparse Core Ops, SparseCore 0:
  87.4 457.1 all-reduce.9
Sparse Core Ops, SparseCore 1:
  549.4 87.8 all-reduce.7
where the time goes:
time: 653 us
  waiting for transfers between devices  567 us (87%)
  other arithmetic  27.4 us (4%)
  starting transfers between devices  23.5 us (4%)
  between operations  17.9 us (3%)
  matrix products  9.94 us (2%)
  local copies, waits for them, and re-layouts  7.28 us (1%)
    psum x1, waiting for transfers between devices, on_device(): g_in, g_out = lax.psum((g_in, g_out), ('ens', 'slab'))  460 us
    psum x1, waiting for transfers between devices, on_device(): summed = lax.psum(returned, 'ens')  83.9 us
    all_to_all x1, waiting for transfers between devices, on_device(): lax.all_to_all(fresh, 'slab', split_axis=1, concat_axis=0, tiled=True)  22.7 us
    all_to_all x1, starting transfers between devices, on_device(): lax.all_to_all(fresh, 'slab', split_axis=1, concat_axis=0, tiled=True)  18.4 us
  transfers between devices with their start and end apart: 4, of which 3 were waited for; matrix products, arithmetic and copies ran while one was open for 2% of the time, Pallas kernels for 0%

commit v1 on v0

--- a/solution.py
+++ b/solution.py
@@ -113,7 +113,7 @@
         jnp.zeros((level_count, lat_local, lon_count), jnp.float32),
     )
     g_in, g_out, back = lax.fori_loop(0, lat_local, per_row, start)
-    g_in, g_out = lax.psum((g_in, g_out), ("ens", "slab"))
+    g_in, g_out = lax.psum(lax.psum((g_in, g_out), "slab"), "ens")
     returned = lax.all_to_all(back, "slab", split_axis=0, concat_axis=1, tiled=True)
     summed = lax.psum(returned, "ens")
     grad_state = diffuse(summed, east, north)

time: 653 us -> 714 us (1.093)
  waiting for transfers between devices: 567 us -> 630 us
    psum x2, waiting for transfers between devices: 544 us -> 607 us  [on_device(): g_in, g_out = lax.psum(lax.psum((g_in, g_out), 'slab'), 'ens')]
  transfers between devices with their start and end apart: 4 -> 4, of which waited for: 3 -> 3; matrix products, arithmetic and copies ran while one was open for 2% -> 1% of each run, Pallas kernels for 0% -> 0%
where the time goes in v1:
time: 714 us; the launch traced here: 713 us
  waiting for transfers between devices  630 us (88%)
  other arithmetic  25.5 us (4%)
  starting transfers between devices  23.5 us (3%)
  between operations  16.5 us (2%)
  matrix products  9.95 us (1%)
  local copies, waits for them, and re-layouts  7.38 us (1%)
    psum x2, waiting for transfers between devices, on_device(): g_in, g_out = lax.psum(lax.psum((g_in, g_out), 'slab'), 'ens')  607 us
    all_to_all x1, waiting for transfers between devices, on_device(): lax.all_to_all(fresh, 'slab', split_axis=1, concat_axis=0, tiled=True)  22.7 us
    all_to_all x1, starting transfers between devices, on_device(): lax.all_to_all(fresh, 'slab', split_axis=1, concat_axis=0, tiled=True)  18.4 us
  transfers between devices with their start and end apart: 4, of which 3 were waited for; matrix products, arithmetic and copies ran while one was open for 1% of the time, Pallas kernels for 0%

profile of v1, /device:TPU:32, one launch (start us, length us, event | category | flops | bytes accessed | tf_op | source)
XLA Modules:
  0.0 713.1 jit_solution(2908997914553234175)
XLA Ops:
  7.2 0.0 copy-start
  7.2 0.0 copy-start.3
  8.0 4.9 fusion.15
  12.9 0.2 slice_subtract_fusion.1
  13.1 0.6 slice.72
  13.7 1.0 fusion.36
  14.7 5.8 fusion.16
  20.5 0.1 slice.74
  20.7 5.2 fusion.18
  25.9 18.4 %all-to-all-start = ((f32[1,64,1024]{2,0,1:T(1,128)}), f32[1,64,1024]{2,0,1:T(1,128)S(1)}, u32[]{:S(2)}, u32[]{:S(2)}) async-start(f32[1,64,1024]{2,0,1:T(1,128)} %fusion.18), calls=%async_computation | async-start | bytes 524288 | tf_op jit(solution)/shard_map/all_to_all | solution.py:80
  44.3 0.1 slice.55
  44.3 0.0 copy-done.8
  44.3 0.1 convert_reduce_fusion
  44.4 22.7 %all-to-all-done = f32[1,64,1024]{2,0,1:T(1,128)S(1)} async-done(((f32[1,64,1024]{2,0,1:T(1,128)}), f32[1,64,1024]{2,0,1:T(1,128)S(1)}, u32[]{:S(2)}, u32[]{:S(2)}) %all-to-all-start) | async-done | bytes 262176 | tf_op jit(solution)/shard_map/all_to_all | solution.py:80
  67.1 0.4 convolution_convert_fusion
  67.6 0.0 copy-start.6
  67.6 0.0 copy-start.7
  67.6 0.0 copy-start.9
  67.6 1.4 multiply_convert_fusion
  69.1 0.8 fusion.5
  69.9 0.5 copy-done.1
  70.4 2.1 fusion.1
  72.5 0.8 fusion.38
  73.3 0.5 convolution_bitcast_fusion
  73.8 1.0 copy.23
  74.8 4.9 all-to-all-start.1
  79.7 0.0 all-reduce.9.cloned.1.call-start
  79.7 2.8 fusion.39
  82.5 1.2 fusion.37
  83.7 0.0 all-reduce.9.cloned.1.call-update
  83.7 0.2 all-reduce.11.cloned.1.call-start
  83.9 518.7 %all-reduce.9.cloned.1.call-done = (f32[64,1024]{1,0:T(8,128)}, f32[1024,64]{0,1:T(8,128)}) async-done(((f32[64,1024]{1,0:T(8,128)}, f32[1024,64]{0,1:T(8,128)}), (f32[64,1024]{1,0:T(8,128)}, f32[1024,64]{0,1:T(8,128)})) %all-reduce.9.cloned.1.call-update) | async-done | bytes 524304 | tf_op jit(solution)/shard_map/psum | solution.py:116
  602.6 0.0 all-to-all-done.1
  602.6 0.7 copy-done.4
  603.3 0.0 all-reduce.11.cloned.1.call-update
  603.3 88.8 %all-reduce.11.cloned.1.call-done = (f32[64,1024]{1,0:T(8,128)}, f32[1024,64]{0,1:T(8,128)}, f32[1,64,1024]{2,0,1:T(1,128)}) async-done(((f32[64,1024]{1,0:T(8,128)}, f32[1024,64]{0,1:T(8,128)}, f32[1,64,1024]{2,0,1:T(1,128)}), (f32[64,1024]{1,0:T(8,128)}, f32[1024,64]{0,1:T(8,128)}, f32[1,64,1024]{2,0,1:T(1,128)})) %all-reduce.11.cloned.1.call-update) | async-done | bytes 786448 | tf_op jit(solution)/shard_map/psum | solution.py:116
  692.1 0.8 slice.80
  693.0 1.3 slice_subtract_fusion
  694.3 1.6 slice.79
  695.9 1.6 multiply_reduce_fusion
  698.2 1.6 multiply_reduce_fusion.1
  700.5 1.7 broadcast_divide_fusion.1
  702.2 0.3 pad_multiply_fusion
  702.5 1.7 broadcast_divide_fusion
  704.2 0.4 fusion.19
  704.6 0.1 slice.81
  704.8 0.7 fusion.21
  705.5 0.8 copy.24
  (23 shorter events, 0.1 us)
Async XLA Ops:
  7.2 60.4 %copy-start = (bf16[64,1024]{1,0:T(8,128)(2,1)S(1)}, bf16[64,1024]{1,0:T(8,128)(2,1)}, u32[]{:S(2)}) copy-start(bf16[64,1024]{1,0:T(8,128)(2,1)} %param.19) | copy-start | bytes 393220
  7.2 13.5 %copy-start.3 = (f32[1,64,1024]{2,1,0:T(8,128)S(1)}, f32[1,64,1024]{2,1,0:T(8,128)}, u32[]{:S(2)}) copy-start(f32[1,64,1024]{2,1,0:T(8,128)} %param.12) | copy-start | bytes 786436
  7.2 37.1 %copy-start.12 = (s32[5]{0:T(128)S(1)}, s32[5]{0:T(128)}, u32[]{:S(2)}) copy-start(s32[5]{0:T(128)} %param.16) | copy-start | bytes 64
  7.2 37.1 %copy-start.8 = (s32[1,1024]{1,0:T(1,128)S(1)}, s32[1,1024]{1,0:T(1,128)}, u32[]{:S(2)}) copy-start(s32[1,1024]{1,0:T(1,128)} %param.17) | copy-start | bytes 12292
  7.2 59.9 %copy-start.5 = (f32[1,64,64]{2,1,0:T(8,128)S(1)}, f32[1,64,64]{2,1,0:T(8,128)}, u32[]{:S(2)}) copy-start(f32[1,64,64]{2,1,0:T(8,128)} %param.15) | copy-start | bytes 49156
  7.2 60.3 %copy-start.10 = (f32[1024]{0:T(1024)S(1)}, f32[1024]{0:T(1024)}, u32[]{:S(2)}) copy-start(f32[1024]{0:T(1024)} %param.21) | copy-start | bytes 12292
  7.2 60.3 %copy-start.11 = (f32[1024]{0:T(1024)S(1)}, f32[1024]{0:T(1024)}, u32[]{:S(2)}) copy-start(f32[1024]{0:T(1024)} %param.20) | copy-start | bytes 12292
  25.9 41.3 %all-to-all-start = ((f32[1,64,1024]{2,0,1:T(1,128)}), f32[1,64,1024]{2,0,1:T(1,128)S(1)}, u32[]{:S(2)}, u32[]{:S(2)}) async-start(f32[1,64,1024]{2,0,1:T(1,128)} %fusion.18), calls=%async_computation | async-start | bytes 524288 | tf_op jit(solution)/shard_map/all_to_all | solution.py:80
  67.6 1.5 copy-start.6
  67.6 1.5 copy-start.7
  67.6 1.5 copy-start.9
  69.1 1.3 copy-start.1
  74.8 527.8 %all-to-all-start.1 = ((f32[64,1,1024]{2,1,0:T(1,128)}), f32[64,1,1024]{2,1,0:T(1,128)S(1)}, u32[]{:S(2)}, u32[]{:S(2)}) async-start(f32[64,1,1024]{2,1,0:T(1,128)} %copy.23), calls=%async_computation.1 | async-start | bytes 524288 | tf_op jit(solution)/shard_map/all_to_all | solution.py:117
  79.7 522.9 %all-reduce.9.cloned.1.call-start = ((), (), s32[]{:S(2)}) async-start(), calls=%async_computation.2 | async-start | bytes 1048576 | tf_op jit(solution)/shard_map/psum | solution.py:116
  83.7 608.4 %all-reduce.11.cloned.1.call-start = ((), (), s32[]{:S(2)}) async-start(), calls=%async_computation.3 | async-start | bytes 1572864 | tf_op jit(solution)/shard_map/psum | solution.py:116
  602.6 0.7 copy-start.4
  692.1 12.0 %copy-start.2 = (f32[1,64,1024]{2,0,1:T(1,128)S(1)}, f32[1,64,1024]{2,0,1:T(1,128)}, u32[]{:S(2)}) copy-start(f32[1,64,1024]{2,0,1:T(1,128)} %get-tuple-element.40) | copy-start | bytes 786436
Sparse Core Ops, SparseCore 0:
  84.0 518.5 all-reduce.8
  606.6 85.4 all-reduce.10

commit v2 on v0

--- a/solution.py
+++ b/solution.py
@@ -115,7 +115,7 @@
     g_in, g_out, back = lax.fori_loop(0, lat_local, per_row, start)
     g_in, g_out = lax.psum((g_in, g_out), ("ens", "slab"))
     returned = lax.all_to_all(back, "slab", split_axis=0, concat_axis=1, tiled=True)
-    summed = lax.psum(returned, "ens")
+    summed = jnp.sum(lax.all_gather(returned, "ens"), axis=0)
     grad_state = diffuse(summed, east, north)
     return (normalized(g_in), normalized(g_out), grad_state)
 

time: 653 us -> 556 us (0.85)
  the two profiles are of different devices: /device:TPU:32 before, /device:TPU:2 now
where the time goes in v2:
time: 556 us
  waiting for transfers between devices  486 us (87%)
  starting transfers between devices  23.7 us (4%)
  between operations  17.9 us (3%)
  other arithmetic  12.6 us (2%)
  matrix products  9.94 us (2%)
  local copies, waits for them, and re-layouts  5.77 us (1%)
    psum x1, waiting for transfers between devices, on_device(): g_in, g_out = lax.psum((g_in, g_out), ('ens', 'slab'))  444 us
    all_to_all x1, waiting for transfers between devices, on_device(): lax.all_to_all(fresh, 'slab', split_axis=1, concat_axis=0, tiled=True)  22.7 us
    all_to_all x1, waiting for transfers between devices, on_device(): lax.all_to_all(back, 'slab', split_axis=0, concat_axis=1, tiled=True)  18.8 us
    all_to_all x1, starting transfers between devices, on_device(): lax.all_to_all(fresh, 'slab', split_axis=1, concat_axis=0, tiled=True)  18.7 us
  transfers between devices with their start and end apart: 4, of which 3 were waited for; matrix products, arithmetic and copies ran while one was open for 2% of the time, Pallas kernels for 0%

profile of v2, /device:TPU:2, one launch (start us, length us, event | category | flops | bytes accessed | tf_op | source)
XLA Modules:
  0.0 555.9 jit_solution(10946490092386185770)
XLA Ops:
  8.0 0.0 copy-start
  8.0 0.0 copy-start.11
  8.0 0.0 copy-start.7
  8.0 0.0 copy-start.4
  8.0 0.0 copy-start.9
  8.1 0.0 copy-start.10
  8.8 1.5 fusion.15
  10.3 0.1 slice.72
  10.5 1.7 convert_multiply_fusion.3
  12.2 0.1 slice.74
  12.2 1.6 fusion.17
  13.8 1.0 copy.24
  14.8 18.7 %all-to-all-start = ((f32[1,64,1024]{2,0,1:T(1,128)}), f32[1,64,1024]{2,0,1:T(1,128)S(1)}, u32[]{:S(2)}, u32[]{:S(2)}) async-start(f32[1,64,1024]{2,0,1:T(1,128)} %copy.24), calls=%async_computation | async-start | bytes 524288 | tf_op jit(solution)/shard_map/all_to_all | solution.py:80
  33.5 0.0 copy-done.11
  33.5 0.1 slice.55
  33.6 0.1 convert_reduce_fusion
  33.7 22.7 %all-to-all-done = f32[1,64,1024]{2,0,1:T(1,128)S(1)} async-done(((f32[1,64,1024]{2,0,1:T(1,128)}), f32[1,64,1024]{2,0,1:T(1,128)S(1)}, u32[]{:S(2)}, u32[]{:S(2)}) %all-to-all-start) | async-done | bytes 262176 | tf_op jit(solution)/shard_map/all_to_all | solution.py:80
  56.4 0.4 convolution_convert_fusion
  56.8 0.0 copy-start.5
  56.9 0.0 copy-start.6
  56.9 0.0 copy-start.8
  56.9 1.4 multiply_convert_fusion
  58.3 0.8 fusion.5
  59.1 0.5 copy-done.1
  59.6 2.1 fusion.1
  61.8 0.8 fusion.36
  62.5 0.5 convolution_bitcast_fusion
  63.0 1.0 copy.25
  64.0 4.9 all-to-all-start.1
  68.9 0.0 all-reduce.7.cloned.1.call-start
  69.0 2.8 fusion.37
  71.8 1.2 fusion.35
  72.9 0.0 all-reduce.7.cloned.1.call-update
  73.0 0.0 all-gather.3.cloned.1.call-start
  73.0 18.8 %all-to-all-done.1 = f32[64,1,1024]{2,1,0:T(1,128)S(1)} async-done(((f32[64,1,1024]{2,1,0:T(1,128)}), f32[64,1,1024]{2,1,0:T(1,128)S(1)}, u32[]{:S(2)}, u32[]{:S(2)}) %all-to-all-start.1) | async-done | bytes 262176 | tf_op jit(solution)/shard_map/all_to_all | solution.py:117
  91.8 0.7 copy-done.3
  92.5 0.0 all-gather.3.cloned.1.call-update
  92.5 444.4 %all-reduce.7.cloned.1.call-done = (f32[64,1024]{1,0:T(8,128)}, f32[1024,64]{0,1:T(8,128)}) async-done(((f32[64,1024]{1,0:T(8,128)}, f32[1024,64]{0,1:T(8,128)}), (f32[64,1024]{1,0:T(8,128)}, f32[1024,64]{0,1:T(8,128)})) %all-reduce.7.cloned.1.call-update) | async-done | bytes 524304 | tf_op jit(solution)/shard_map/psum | solution.py:116
  537.0 1.6 multiply_reduce_fusion
  539.3 1.6 multiply_reduce_fusion.1
  541.6 1.7 broadcast_divide_fusion.1
  543.3 1.7 broadcast_divide_fusion
  545.0 2.1 copy.27
  547.1 0.1 reduce.1
  547.3 0.1 slice.79
  547.4 0.1 convert_multiply_fusion.2
  547.5 0.1 slice.81
  547.6 0.8 fusion.19
  (19 shorter events, 0.1 us)
Async XLA Ops:
  8.0 48.8 %copy-start = (bf16[64,1024]{1,0:T(8,128)(2,1)S(1)}, bf16[64,1024]{1,0:T(8,128)(2,1)}, u32[]{:S(2)}) copy-start(bf16[64,1024]{1,0:T(8,128)(2,1)} %param.19) | copy-start | bytes 393220
  8.0 25.5 %copy-start.11 = (s32[5]{0:T(128)S(1)}, s32[5]{0:T(128)}, u32[]{:S(2)}) copy-start(s32[5]{0:T(128)} %param.16) | copy-start | bytes 64
  8.0 25.6 %copy-start.7 = (s32[1,1024]{1,0:T(1,128)S(1)}, s32[1,1024]{1,0:T(1,128)}, u32[]{:S(2)}) copy-start(s32[1,1024]{1,0:T(1,128)} %param.17) | copy-start | bytes 12292
  8.0 48.4 %copy-start.4 = (f32[1,64,64]{2,1,0:T(8,128)S(1)}, f32[1,64,64]{2,1,0:T(8,128)}, u32[]{:S(2)}) copy-start(f32[1,64,64]{2,1,0:T(8,128)} %param.15) | copy-start | bytes 49156
  8.0 48.8 %copy-start.9 = (f32[1024]{0:T(1024)S(1)}, f32[1024]{0:T(1024)}, u32[]{:S(2)}) copy-start(f32[1024]{0:T(1024)} %param.21) | copy-start | bytes 12292
  8.1 48.8 %copy-start.10 = (f32[1024]{0:T(1024)S(1)}, f32[1024]{0:T(1024)}, u32[]{:S(2)}) copy-start(f32[1024]{0:T(1024)} %param.20) | copy-start | bytes 12292
  14.8 41.6 %all-to-all-start = ((f32[1,64,1024]{2,0,1:T(1,128)}), f32[1,64,1024]{2,0,1:T(1,128)S(1)}, u32[]{:S(2)}, u32[]{:S(2)}) async-start(f32[1,64,1024]{2,0,1:T(1,128)} %copy.24), calls=%async_computation | async-start | bytes 524288 | tf_op jit(solution)/shard_map/all_to_all | solution.py:80
  56.8 1.5 copy-start.5
  56.9 1.5 copy-start.6
  56.9 1.5 copy-start.8
  58.3 1.3 copy-start.1
  64.0 27.8 %all-to-all-start.1 = ((f32[64,1,1024]{2,1,0:T(1,128)}), f32[64,1,1024]{2,1,0:T(1,128)S(1)}, u32[]{:S(2)}, u32[]{:S(2)}) async-start(f32[64,1,1024]{2,1,0:T(1,128)} %copy.25), calls=%async_computation.1 | async-start | bytes 524288 | tf_op jit(solution)/shard_map/all_to_all | solution.py:117
  68.9 468.0 %all-reduce.7.cloned.1.call-start = ((), (), s32[]{:S(2)}) async-start(), calls=%async_computation.3 | async-start | bytes 1048576 | tf_op jit(solution)/shard_map/psum | solution.py:116
  73.0 472.0 %all-gather.3.cloned.1.call-start = ((), (), s32[]{:S(2)}) async-start(), calls=%async_computation.2 | async-start | bytes 2359296 | tf_op jit(solution)/shard_map/all_gather | solution.py:118
  91.8 0.7 copy-start.3
  543.3 4.1 copy-start.2
Sparse Core Ops, SparseCore 0:
  75.8 461.0 all-reduce.6
Sparse Core Ops, SparseCore 1:
  92.6 37.7 all-gather.2
